TPU v7x, 256 devices: a whole 4x4x8 slice. The times are simulated.
256 devices in a mesh: pop: 16 (over y, x), mp: 16 (over z, core).
Axes of the slice: x: 4, y: 4, z: 8, core: 2. Of those that a mesh axis runs over, the one named last changes fastest.
Arguments:
- tokens: bfloat16 [12288, 4096], P('pop', 'mp'), may hold values from -6 to 6
- weight: bfloat16 [4096, 16384], P('pop', 'mp'), may hold values from -6 to 6
- fitness: float32 [384], P('pop'), may hold values from 0.4 to 14.4
- row_factors: bfloat16 [384, 4096], P('pop'), may hold values from -6 to 6
- col_factors: bfloat16 [384, 16384], P('pop', 'mp'), may hold values from -6 to 6
Outputs:
- keys: bfloat16 [12288, 16384], P('pop', 'mp')
- new_weight: bfloat16 [4096, 16384], P('pop', 'mp')
All inputs are finite; a program needn't handle non-finite values.
Results may differ from a plain program's by a relative error of at most 0.005.
Values may be sent and summed in bfloat16 or wider, within the bound.
A program may use at most 64 MiB of HBM per device.

v0:
```python
import math

import jax
import jax.numpy as jnp
from jax import lax
from jax.experimental import pallas as pl
from jax.experimental.pallas import tpu as pltpu
from jax.sharding import PartitionSpec as P

D = 4096
N = 4
NZ = 8
POP = N * N
MEMB = 24
TOK = 32
ROWS = MEMB * TOK
FEAT = 256
HID = 1024
HALF = HID // 2
COUNT = POP * MEMB
MESH = pl.DeviceIdType.MESH

ORDER = (
    ("C", 1, 0, 0), ("C", 3, 0, 0), ("C", 0, 1, 0), ("C", 0, 3, 0),
    ("I",), ("Z",), ("R",),
    ("W", 1, 0, 0), ("W", 3, 0, 1), ("W", 0, 1, 0), ("W", 0, 3, 1),
    ("C", 2, 0, 0), ("C", 2, 0, 1), ("C", 1, 1, 0), ("C", 1, 3, 0),
    ("C", 3, 1, 0), ("C", 3, 3, 0), ("C", 0, 2, 0), ("C", 0, 2, 1),
    ("T", 1, 0),
    ("W", 3, 0, 0), ("W", 1, 0, 1), ("W", 0, 1, 1), ("W", 0, 3, 0),
    ("T", 1, 1),
    ("W", 2, 0, 1), ("W", 2, 0, 0),
    ("T", 2, 0), ("S", 1),
    ("W", 1, 1, 0), ("W", 1, 3, 0), ("W", 3, 1, 1), ("W", 3, 3, 1),
    ("T", 2, 1),
    ("W", 0, 2, 0), ("W", 0, 2, 1),
    ("C", 2, 1, 0), ("C", 2, 3, 0), ("C", 1, 2, 1), ("C", 1, 2, 0),
    ("C", 3, 2, 1), ("C", 3, 2, 0),
    ("S", 2), ("A", 0), ("A", 2), ("A", 4),
    ("T", 3, 0),
    ("A", 6), ("A", 8), ("A", 10),
    ("W", 3, 3, 0), ("W", 3, 1, 0), ("A", 12), ("A", 14), ("W", 1, 3, 1), ("W", 1, 1, 1),
    ("T", 3, 1), ("S", 3), ("E", 0),
    ("W", 2, 3, 1), ("W", 2, 1, 1), ("E", 2), ("E", 4),
    ("T", 4, 0), ("E", 6), ("E", 8),
    ("W", 2, 3, 0), ("W", 2, 1, 0), ("E", 10), ("E", 12), ("E", 14), ("S", 4), ("K",),
    ("W", 3, 2, 1), ("W", 1, 2, 0),
    ("G", 2, 1), ("G", 2, 3),
    ("C", 2, 2, 1), ("C", 2, 2, 0),
    ("W", 1, 2, 1), ("W", 3, 2, 0),
    ("D",),
    ("G", 1, 2), ("G", 3, 2),
)


def kernel(tok, w, fit, row_in, col_in, keys, neww,
           row, col, wbuf, tbuf, cbuf, rbuf, rsrc, csrc, rowf, colf, shp, scaled, rfull,
           acc, pacc, ssem, rsem, lsem, ready):
    p, m = lax.axis_index("pop"), lax.axis_index("mp")
    x, y, z, c = lax.rem(p, N), lax.div(p, N), lax.div(m, 2), lax.rem(m, 2)
    a, b = x * (1 - c) + y * c, y * (1 - c) + x * c

    def group(ga, gb):
        ga, gb = lax.rem(ga, N), lax.rem(gb, N)
        return (gb * (1 - c) + ga * c) * N + ga * (1 - c) + gb * c

    def plane(dz, dc=0):
        return lax.rem(z + dz + NZ, NZ) * 2 + lax.rem(c + dc, 2)

    src = {(i, j): group(a + N - i, b + N - j) for i in range(N) for j in range(N)}
    links = {
        "a+": (group(a + 1, b), m), "a-": (group(a + 3, b), m),
        "b+": (group(a, b + 1), m), "b-": (group(a, b + 3), m),
        "z+": (p, plane(1)), "z-": (p, plane(-1)), "s": (p, plane(0, 1)),
    }
    far = [(i, j) for i in range(N) for j in range(N) if (i, j) != (0, 0)]

    def own_w(half):
        return w.at[:, pl.ds(half * HALF, HALF)]

    loads = [
        pltpu.make_async_copy(col_in, col, lsem.at[0]),
        pltpu.make_async_copy(row_in, row, lsem.at[1]),
        pltpu.make_async_copy(own_w(0), wbuf.at[p, 0], lsem.at[2]),
        pltpu.make_async_copy(own_w(1), wbuf.at[p, 1], lsem.at[3]),
        pltpu.make_async_copy(tok, tbuf.at[m], lsem.at[4]),
    ]
    for copy in loads:
        copy.start()

    barrier = pltpu.get_barrier_semaphore()

    def signal(sem, dev):
        pl.semaphore_signal(sem, inc=1, device_id=dev, device_id_type=MESH)

    signal(barrier, links["s"])
    for link in ("a+", "a-", "b+", "b-"):
        signal(barrier, (links[link][0], 2 * z))
    for q in range(2):
        @pl.when(p != 2 * z + q)
        def _(q=q):
            signal(barrier, (2 * z + q, 2 * z))
    for dz in (1, -1):
        signal(barrier, (p, lax.rem(z + dz + NZ, NZ) * 2 + 1))
    source = jnp.where(lax.div(p, 2) == z, 1, 0)

    loads[0].wait()
    colv = col[...].astype(jnp.float32)
    colf[0] = colv[:, :HALF]
    colf[1] = colv[:, HALF:]
    own_col = jnp.concatenate([colv[:, :HALF], colv[:, HALF:]], axis=0).astype(jnp.bfloat16)
    csrc[...] = own_col
    cbuf[p] = own_col

    @pl.when(c == 0)
    def _():
        pl.semaphore_wait(barrier, 9 + 30 * source)
        signal(ready.at[0], links["s"])

    @pl.when(c == 1)
    def _():
        pl.semaphore_wait(ready.at[0], 1)

    copies = {}

    def send(key, source, target, dev):
        n = len(copies)
        copy = pltpu.make_async_remote_copy(
            src_ref=source, dst_ref=target, send_sem=ssem.at[n], recv_sem=rsem.at[n],
            device_id=dev, device_id_type=MESH,
        )
        copy.start()
        copies[key] = copy

    def send_w(link, key, half, source=None):
        slot = src[back(key, link)]
        source = wbuf.at[slot, half] if source is None else source
        send(("W", *key, half), source, wbuf.at[slot, half], links[link])

    def back(key, link):
        i, j = key
        step = {"a+": (1, 0), "a-": (3, 0), "b+": (0, 1), "b-": (0, 3)}[link]
        return ((i - step[0]) % N, (j - step[1]) % N)

    def send_c(link, key, part, lo=0, rows=2 * MEMB):
        slot = src[back(key, link)]
        source = csrc if back(key, link) == (0, 0) else cbuf.at[slot]
        send(("C", *key, part), source.at[pl.ds(lo, rows)], cbuf.at[slot, pl.ds(lo, rows)], links[link])

    send_c("a+", (1, 0), 0)
    send_c("a-", (3, 0), 0)
    send_c("b+", (0, 1), 0)
    send_c("b-", (0, 3), 0)
    send_w("a+", (1, 0), 0, own_w(0))
    send_w("a-", (3, 0), 1, own_w(1))
    send_w("b+", (0, 1), 0, own_w(0))
    send_w("b-", (0, 3), 1, own_w(1))

    send(("S", 0), tok, tbuf.at[m], links["s"])

    loads[1].wait()
    for q in range(POP):
        rowf[q] = row[:, q * FEAT:(q + 1) * FEAT].astype(jnp.float32)

    def pieces(some=far):
        return [
            pltpu.make_async_remote_copy(
                src_ref=rsrc.at[group(a + i, b + j)], dst_ref=rbuf.at[m],
                send_sem=ssem.at[120 + n], recv_sem=rsem.at[120],
                device_id=(group(a + i, b + j), m), device_id_type=MESH,
            )
            for n, (i, j) in enumerate(some)
        ]

    @pl.when(p == m)
    def _():
        lane = lax.broadcasted_iota(jnp.int32, (8, FEAT), 1)
        sub = lax.broadcasted_iota(jnp.int32, (8, FEAT), 0)
        value = jnp.zeros((8, FEAT), jnp.float32)
        for i in range(MEMB):
            value = jnp.where(lane == i, fit[i], value)
        high = value.astype(jnp.bfloat16).astype(jnp.float32)
        middle = (value - high).astype(jnp.bfloat16).astype(jnp.float32)
        low = value - high - middle
        tile = jnp.where(sub == 0, high, jnp.where(sub == 1, middle, jnp.where(sub == 2, low, 0.0)))
        for q in range(POP):
            rsrc[q] = jnp.concatenate([rowf[q], tile], axis=0).astype(jnp.bfloat16)
        for copy in pieces():
            copy.start()
        rbuf[m] = rsrc[p]

    pacc[...] = jnp.zeros_like(pacc)
    acc[...] = jnp.zeros_like(acc)
    for copy in loads[2:]:
        copy.wait()

    def project(blocks):
        @pl.loop(0, MEMB)
        def _(k):
            rows = pl.ds(pl.multiple_of(k * TOK, TOK), TOK)
            total = pacc[rows, :]
            for f in blocks:
                term = tbuf[f, rows, :].astype(jnp.float32) * rowf[f, pl.ds(k, 1), :]
                total = total + (term[:, :128] + term[:, 128:])
            pacc[rows, :] = total

    def half(k):
        return pl.ds(k * (ROWS // 2), ROWS // 2)

    def send_t(dz, k, f=None):
        f = m if f is None else f
        source = tok if abs(dz) == 1 else tbuf.at[f]
        send(("T", dz, k), source.at[half(k)], tbuf.at[f, half(k)], links["z+" if dz > 0 else "z-"])

    def take_t(d, turn):
        for way in (1, -1):
            dz, k = d * way, turn if way > 0 else 1 - turn
            f = plane(-dz)
            copies["T", dz, k].wait_recv()
            if d < 3 or (d == 3 and turn == 0):
                send_t(dz + way, k, f)
            send(("S", dz, k), tbuf.at[f, half(k)], tbuf.at[f, half(k)], links["s"])
            if turn == 1 or (d == 4 and way > 0):
                copies["R", dz].wait_recv()
                if d < 3 or (d == 3 and way > 0):
                    send(("R", dz + way), rbuf.at[f], rbuf.at[f], links["z+" if way > 0 else "z-"])
                send(("Q", dz), rbuf.at[f], rbuf.at[f], links["s"])

    def take_s(d):
        if d == 1:
            copies["S", 0].wait_recv()
            project([m, plane(0, 1)])
        if d < 4:
            for dz in (d, -d):
                for k in range(2):
                    copies["S", dz, k].wait_recv()
            project([plane(-dz, dc) for dz in (d, -d) for dc in (0, 1)])
        else:
            copies["S", 4, 0].wait_recv()
            copies["S", -4, 1].wait_recv()
            project([plane(4), plane(4, 1)])

            @pl.loop(0, MEMB)
            def _(k):
                rows = pl.ds(pl.multiple_of(k * TOK, TOK), TOK)
                proj = 0.3 * jnp.sum(pacc[rows, :], axis=1, keepdims=True)
                for s in range(2):
                    acc[s, rows, :] += proj * colf[s, pl.ds(k, 1), :]

    def take_w(i, j, s):
        copies["W", i, j, s].wait_recv()
        if j == 0:
            if (i, s) == (1, 0):
                send_w("a+", (2, 0), 0)
            if (i, s) == (3, 1):
                send_w("a-", (2, 0), 1)
            send_w("b+", (i, 1), s)
            send_w("b-", (i, 3), s)
        elif (j, s) == (1, 0):
            send_w("b+", (i, 2), 0)
        elif (j, s) == (3, 1):
            send_w("b-", (i, 2), 1)

    def take_c(i, j, part):
        copies["C", i, j, part].wait_recv()
        if j == 0:
            if i == 1:
                send_c("a+", (2, 0), 0, 0, 32)
            if i == 3:
                send_c("a-", (2, 0), 1, 32, 16)
            if i != 2 or part == 1:
                send_c("b+", (i, 1), 0)
                send_c("b-", (i, 3), 0)
        elif j == 1:
            send_c("b+", (i, 2), 0, 0, 16 if i in (0, 2) else 32)
        elif j == 3:
            lo = 16 if i in (0, 2) else 32
            send_c("b-", (i, 2), 1, lo, 48 - lo)

    def gather(f):
        for s in range(2):
            acc[s] += jnp.dot(tbuf[f], wbuf[f, s], preferred_element_type=jnp.float32)

    def place(f):
        fx, fy = lax.rem(f, N), lax.div(f, N)
        i = lax.rem(a + N - (fx * (1 - c) + fy * c), N)
        j = lax.rem(b + N - (fy * (1 - c) + fx * c), N)
        dz = lax.rem(lax.div(f, 2) + NZ - z, NZ)
        return i, j, jnp.minimum(dz, NZ - dz)

    def early(f):
        i, j, _ = place(f)
        return (i == 0) | (j == 0) | ((i != 2) & (j != 2))

    def first(f):
        i, j, d = place(f)
        return (((i == 0) & (j != 2)) | (j == 0)) & (d <= 2)

    def gather_first(start):
        @pl.loop(start, start + 2)
        def _(f):
            @pl.when(first(f))
            def _():
                gather(f)

    def gather_near(start):
        @pl.loop(start, start + 2)
        def _(f):
            @pl.when(early(f) & jnp.logical_not(first(f)) & (place(f)[2] <= 3))
            def _():
                gather(f)

    def gather_far():
        for dc in range(2):
            f = plane(4, dc)

            @pl.when(early(f))
            def _(f=f):
                gather(f)

    def start_z():
        @pl.when(c == 1)
        def _():
            pl.semaphore_wait(barrier, 5)
            signal(ready.at[1], links["s"])

        @pl.when(c == 0)
        def _():
            pl.semaphore_wait(ready.at[1], 1)

        for turn in range(2):
            send_t(1, turn)
            send_t(-1, 1 - turn)

    def start_r():
        @pl.when(p != m)
        def _():
            pieces(far[:1])[0].wait_recv()

        for dz, link in ((1, "z+"), (-1, "z-")):
            send(("R", dz), rbuf.at[m], rbuf.at[m], links[link])
        send(("Q", 0), rbuf.at[m], rbuf.at[m], links["s"])

    def rest_of_own():
        send_w("a+", (1, 0), 1, own_w(1))
        send_w("a-", (3, 0), 0, own_w(0))
        send_w("b+", (0, 1), 1, own_w(1))
        send_w("b-", (0, 3), 0, own_w(0))

    def delta():
        for dz in (0, 1, -1, 2, -2, 3, -3, 4):
            copies["Q", dz].wait_recv()
        diagonal = lax.broadcasted_iota(jnp.int32, (MEMB, 128), 0) == lax.broadcasted_iota(jnp.int32, (MEMB, 128), 1)
        sums = jnp.zeros((1, 128), jnp.float32)
        squares = jnp.zeros((1, 128), jnp.float32)
        for q in range(POP):
            piece = rbuf[q].astype(jnp.float32)
            rfull[q * MEMB:(q + 1) * MEMB, :] = piece[:MEMB]
            tail = piece[MEMB:, :128]
            value = (tail[0:1] + tail[1:2]) + tail[2:3]
            sums += value
            squares += value * value
            column = jnp.sum(jnp.where(diagonal, value, 0.0), axis=1, keepdims=True)
            shp[q] = jnp.broadcast_to(column, (MEMB, 128))
        mean = jnp.sum(sums, axis=1, keepdims=True) / COUNT
        var = jnp.sum(squares, axis=1, keepdims=True) / COUNT - mean * mean
        scale = jnp.sqrt(var + 1e-05)

        @pl.loop(0, POP // 2)
        def _(t):
            out = pl.ds(pl.multiple_of(t * 48, 48), 48)
            two = (2 * t, 2 * t + 1)
            for h in range(2):
                part = slice(h * MEMB, (h + 1) * MEMB)
                scaled[h, out, :] = jnp.concatenate(
                    [(shp[q][:, 0:1] - mean) / scale * cbuf[q].astype(jnp.float32)[part] / math.sqrt(COUNT) for q in two],
                    axis=0,
                ).astype(jnp.bfloat16)
        left = jnp.transpose(rfull[...]).astype(jnp.bfloat16)
        for h in range(2):
            part = slice(h * HALF, (h + 1) * HALF)
            d = jnp.dot(left, scaled[h], preferred_element_type=jnp.float32)
            neww[:, part] = (wbuf[p, h].astype(jnp.float32) + 0.5 * d).astype(jnp.bfloat16)

    steps = {
        "W": take_w, "C": take_c, "T": take_t, "I": rest_of_own, "Z": start_z, "R": start_r,
        "A": gather_first, "E": gather_near, "K": gather_far, "G": lambda i, j: gather(src[i, j]), "D": delta, "S": take_s,
    }
    for step in ORDER:
        steps[step[0]](*step[1:])
    for s in (1, 0):
        copies["W", 2, 2, s].wait_recv()

        f = src[2, 2]
        h = (acc[s] + jnp.dot(tbuf[f], wbuf[f, s], preferred_element_type=jnp.float32)) / math.sqrt(D)
        keys[:, s * HALF:(s + 1) * HALF] = (jnp.maximum(h, 0.0) ** 2).astype(jnp.bfloat16)

    for copy in copies.values():
        copy.wait_send()

    @pl.when(p == m)
    def _():
        for copy in pieces():
            copy.wait_send()


def local(tokens, weight, fitness, row_factors, col_factors):
    hbm = pl.BlockSpec(memory_space=pl.ANY)
    vmem = pl.BlockSpec(memory_space=pltpu.VMEM)
    bf, f32 = jnp.bfloat16, jnp.float32
    return pl.pallas_call(
        kernel,
        out_shape=(pltpu.VMEM((ROWS, HID), bf), pltpu.VMEM((FEAT, HID), bf)),
        in_specs=[hbm, hbm, pl.BlockSpec(memory_space=pltpu.SMEM), hbm, hbm],
        out_specs=(vmem, vmem),
        scratch_shapes=[
            pltpu.VMEM((MEMB, D), bf),
            pltpu.VMEM((MEMB, HID), bf),
            pltpu.VMEM((POP, 2, FEAT, HALF), bf),
            pltpu.VMEM((2 * NZ, ROWS, FEAT), bf),
            pltpu.VMEM((POP, 2 * MEMB, HALF), bf),
            pltpu.VMEM((POP, 32, FEAT), bf),
            pltpu.VMEM((POP, 32, FEAT), bf),
            pltpu.VMEM((2 * MEMB, HALF), bf),
            pltpu.VMEM((POP, MEMB, FEAT), f32),
            pltpu.VMEM((2, MEMB, HALF), f32),
            pltpu.VMEM((POP, MEMB, 128), f32),
            pltpu.VMEM((2, COUNT, HALF), bf),
            pltpu.VMEM((COUNT, FEAT), f32),
            pltpu.VMEM((2, ROWS, HALF), f32),
            pltpu.VMEM((ROWS, 128), f32),
            pltpu.SemaphoreType.DMA((135,)),
            pltpu.SemaphoreType.DMA((121,)),
            pltpu.SemaphoreType.DMA((5,)),
            pltpu.SemaphoreType.REGULAR((2,)),
        ],
        compiler_params=pltpu.CompilerParams(
            collective_id=0, has_side_effects=True, vmem_limit_bytes=57 << 20
        ),
        cost_estimate=pl.CostEstimate(flops=6_700_000_000, bytes_accessed=4_000_000, transcendentals=0),
    )(tokens, weight, fitness, row_factors, col_factors)


def solution(mesh):
    placed = (P("pop", "mp"), P("pop", "mp"), P("pop"), P("pop", None), P("pop", "mp"))
    return jax.shard_map(
        local,
        mesh=mesh,
        in_specs=placed,
        out_specs=(P("pop", "mp"), P("pop", "mp")),
        check_vma=False,
    )
```

profile of v0, /device:TPU:1, one launch (start us, length us, event | category | flops | bytes accessed | tf_op | source)
XLA Modules:
  0.0 63.0 jit_solution(4173953526415168280)
XLA Ops:
  0.6 60.5 %shard_map.68 = (bf16[768,1024]{1,0:T(8,128)(2,1)S(1)}, bf16[256,1024]{1,0:T(8,128)(2,1)S(1)}) custom-call(bf16[768,256]{1,0:T(8,128)(2,1)} %tok.1, bf16[256,1024]{1,0:T(8,128)(2,1)} %w.1, f32[24]{0:T(128)} %fit.1, bf16[24,4096]{1,0:T(8,128)(2,1)} %row_in.1, bf16[24,1024]{1,0:T(8,128)(2,1)} %col_in.1), custom_call_target="tpu_custom_call" | custom-call | flops 6700000256 | bytes 4000000 | tf_op jit(solution)/shard_map/pallas_call | solution.py:411
  61.1 1.1 %copy.9 = bf16[768,1024]{1,0:T(8,128)(2,1)} copy(bf16[768,1024]{1,0:T(8,128)(2,1)S(1)} %get-tuple-element.2) | data formatting | bytes 3145728
  62.2 0.8 %copy.10 = bf16[256,1024]{1,0:T(8,128)(2,1)} copy(bf16[256,1024]{1,0:T(8,128)(2,1)S(1)} %get-tuple-element.3) | data formatting | bytes 1048576
where the time goes:
time: 63.1 us; the launch traced here: 63 us
  Pallas kernels  60.5 us (96%)
  local copies, waits for them, and re-layouts  1.94 us (3%)
  between operations  0.64 us (1%)
    pallas_call x1, Pallas kernels, local(): pl.pallas_call(kernel, out_shape=(pltpu.VMEM((ROWS, HID), bf), pltpu.VMEM...  60.5 us
    unnamed x2, local copies, waits for them, and re-layouts  1.94 us

commit v1 on v0

--- a/solution.py
+++ b/solution.py
@@ -21,35 +21,18 @@
 MESH = pl.DeviceIdType.MESH
 
 ORDER = (
-    ("C", 1, 0, 0), ("C", 3, 0, 0), ("C", 0, 1, 0), ("C", 0, 3, 0),
-    ("I",), ("Z",), ("R",),
-    ("W", 1, 0, 0), ("W", 3, 0, 1), ("W", 0, 1, 0), ("W", 0, 3, 1),
-    ("C", 2, 0, 0), ("C", 2, 0, 1), ("C", 1, 1, 0), ("C", 1, 3, 0),
-    ("C", 3, 1, 0), ("C", 3, 3, 0), ("C", 0, 2, 0), ("C", 0, 2, 1),
-    ("T", 1, 0),
-    ("W", 3, 0, 0), ("W", 1, 0, 1), ("W", 0, 1, 1), ("W", 0, 3, 0),
-    ("T", 1, 1),
-    ("W", 2, 0, 1), ("W", 2, 0, 0),
-    ("T", 2, 0), ("S", 1),
-    ("W", 1, 1, 0), ("W", 1, 3, 0), ("W", 3, 1, 1), ("W", 3, 3, 1),
-    ("T", 2, 1),
-    ("W", 0, 2, 0), ("W", 0, 2, 1),
-    ("C", 2, 1, 0), ("C", 2, 3, 0), ("C", 1, 2, 1), ("C", 1, 2, 0),
-    ("C", 3, 2, 1), ("C", 3, 2, 0),
-    ("S", 2), ("A", 0), ("A", 2), ("A", 4),
-    ("T", 3, 0),
-    ("A", 6), ("A", 8), ("A", 10),
-    ("W", 3, 3, 0), ("W", 3, 1, 0), ("A", 12), ("A", 14), ("W", 1, 3, 1), ("W", 1, 1, 1),
-    ("T", 3, 1), ("S", 3), ("E", 0),
-    ("W", 2, 3, 1), ("W", 2, 1, 1), ("E", 2), ("E", 4),
-    ("T", 4, 0), ("E", 6), ("E", 8),
-    ("W", 2, 3, 0), ("W", 2, 1, 0), ("E", 10), ("E", 12), ("E", 14), ("S", 4), ("K",),
-    ("W", 3, 2, 1), ("W", 1, 2, 0),
-    ("G", 2, 1), ("G", 2, 3),
-    ("C", 2, 2, 1), ("C", 2, 2, 0),
-    ("W", 1, 2, 1), ("W", 3, 2, 0),
-    ("D",),
-    ("G", 1, 2), ("G", 3, 2),
+    ("C", 1, 0, 0), ("C", 3, 0, 0), ("C", 0, 1, 0), ("C", 0, 3, 0), ("I",), ("Z",), ("R",), ("W", 1, 0, 0),
+    ("W", 3, 0, 1), ("W", 0, 1, 0), ("W", 0, 3, 1), ("C", 2, 0, 0), ("C", 2, 0, 1), ("C", 1, 1, 0),
+    ("C", 1, 3, 0), ("C", 3, 1, 0), ("C", 3, 3, 0), ("C", 0, 2, 0), ("C", 0, 2, 1), ("T", 1, 0),
+    ("W", 3, 0, 0), ("W", 1, 0, 1), ("W", 0, 1, 1), ("T", 1, 1), ("W", 0, 3, 0), ("S", 1), ("W", 2, 0, 1),
+    ("W", 2, 0, 0), ("T", 2, 0), ("W", 1, 1, 0), ("W", 1, 3, 0), ("W", 3, 1, 1), ("W", 3, 3, 1), ("T", 2, 1),
+    ("W", 0, 2, 0), ("W", 0, 2, 1), ("S", 2), ("A", 0), ("C", 2, 1, 0), ("C", 2, 3, 0), ("C", 1, 2, 1),
+    ("C", 1, 2, 0), ("C", 3, 2, 1), ("A", 2), ("C", 3, 2, 0), ("A", 4), ("T", 3, 0), ("A", 6), ("W", 3, 3, 0),
+    ("A", 8), ("W", 3, 1, 0), ("A", 10), ("A", 12), ("W", 1, 3, 1), ("A", 14), ("T", 3, 1), ("W", 1, 1, 1),
+    ("B", 0), ("B", 2), ("B", 4), ("S", 3), ("B", 6), ("W", 2, 3, 1), ("B", 8), ("W", 2, 1, 1), ("B", 10),
+    ("B", 12), ("T", 4, 0), ("B", 14), ("K", 3), ("W", 2, 3, 0), ("W", 2, 1, 0), ("K", -3), ("S", 4),
+    ("K", 4), ("G", 2, 1), ("W", 3, 2, 1), ("W", 1, 2, 0), ("C", 2, 2, 1), ("G", 2, 3), ("C", 2, 2, 0),
+    ("D",), ("W", 1, 2, 1), ("W", 3, 2, 0), ("G", 1, 2), ("G", 3, 2),
 )
 
 
@@ -112,6 +95,9 @@
     csrc[...] = own_col
     cbuf[p] = own_col
 
+    for copy in loads[2:]:
+        copy.wait()
+
     @pl.when(c == 0)
     def _():
         pl.semaphore_wait(barrier, 9 + 30 * source)
@@ -134,7 +120,7 @@
 
     def send_w(link, key, half, source=None):
         slot = src[back(key, link)]
-        source = wbuf.at[slot, half] if source is None else source
+        source = wbuf.at[slot, half]
         send(("W", *key, half), source, wbuf.at[slot, half], links[link])
 
     def back(key, link):
@@ -156,7 +142,7 @@
     send_w("b+", (0, 1), 0, own_w(0))
     send_w("b-", (0, 3), 1, own_w(1))
 
-    send(("S", 0), tok, tbuf.at[m], links["s"])
+    send(("S", 0), tbuf.at[m], tbuf.at[m], links["s"])
 
     loads[1].wait()
     for q in range(POP):
@@ -191,8 +177,6 @@
 
     pacc[...] = jnp.zeros_like(pacc)
     acc[...] = jnp.zeros_like(acc)
-    for copy in loads[2:]:
-        copy.wait()
 
     def project(blocks):
         @pl.loop(0, MEMB)
@@ -209,7 +193,7 @@
 
     def send_t(dz, k, f=None):
         f = m if f is None else f
-        source = tok if abs(dz) == 1 else tbuf.at[f]
+        source = tbuf.at[f]
         send(("T", dz, k), source.at[half(k)], tbuf.at[f, half(k)], links["z+" if dz > 0 else "z-"])
 
     def take_t(d, turn):
@@ -293,29 +277,30 @@
         return (i == 0) | (j == 0) | ((i != 2) & (j != 2))
 
     def first(f):
-        i, j, d = place(f)
-        return (((i == 0) & (j != 2)) | (j == 0)) & (d <= 2)
+        i, j, _ = place(f)
+        return ((i == 0) & (j != 2)) | (j == 0)
 
     def gather_first(start):
         @pl.loop(start, start + 2)
         def _(f):
-            @pl.when(first(f))
+            @pl.when(first(f) & (place(f)[2] <= 2))
             def _():
                 gather(f)
 
-    def gather_near(start):
+    def gather_next(start):
         @pl.loop(start, start + 2)
         def _(f):
-            @pl.when(early(f) & jnp.logical_not(first(f)) & (place(f)[2] <= 3))
+            @pl.when(early(f) & jnp.logical_not(first(f)) & (place(f)[2] <= 2))
             def _():
                 gather(f)
 
-    def gather_far():
-        for dc in range(2):
-            f = plane(4, dc)
+    def gather_far(dz):
+        @pl.loop(0, 2)
+        def _(dc):
+            f = plane(dz, dc)
 
             @pl.when(early(f))
-            def _(f=f):
+            def _():
                 gather(f)
 
     def start_z():
@@ -384,7 +369,7 @@
 
     steps = {
         "W": take_w, "C": take_c, "T": take_t, "I": rest_of_own, "Z": start_z, "R": start_r,
-        "A": gather_first, "E": gather_near, "K": gather_far, "G": lambda i, j: gather(src[i, j]), "D": delta, "S": take_s,
+        "A": gather_first, "B": gather_next, "K": gather_far, "G": lambda i, j: gather(src[i, j]), "D": delta, "S": take_s,
     }
     for step in ORDER:
         steps[step[0]](*step[1:])

time: 63.1 us -> 62.8 us (level)
  no operation moved by 1% of the time
where the time goes in v1:
time: 62.8 us; the launch traced here: 62.7 us
  Pallas kernels  60.1 us (96%)
  local copies, waits for them, and re-layouts  1.94 us (3%)
  between operations  0.64 us (1%)
    pallas_call x1, Pallas kernels, local(): pl.pallas_call(kernel, out_shape=(pltpu.VMEM((ROWS, HID), bf), pltpu.VMEM...  60.1 us
    unnamed x2, local copies, waits for them, and re-layouts  1.94 us

profile of v1, /device:TPU:1, one launch (start us, length us, event | category | flops | bytes accessed | tf_op | source)
XLA Modules:
  0.0 62.7 jit_solution(3125777417362555341)
XLA Ops:
  0.6 60.1 %shard_map.68 = (bf16[768,1024]{1,0:T(8,128)(2,1)S(1)}, bf16[256,1024]{1,0:T(8,128)(2,1)S(1)}) custom-call(bf16[768,256]{1,0:T(8,128)(2,1)} %tok.1, bf16[256,1024]{1,0:T(8,128)(2,1)} %w.1, f32[24]{0:T(128)} %fit.1, bf16[24,4096]{1,0:T(8,128)(2,1)} %row_in.1, bf16[24,1024]{1,0:T(8,128)(2,1)} %col_in.1), custom_call_target="tpu_custom_call" | custom-call | flops 6700000256 | bytes 4000000 | tf_op jit(solution)/shard_map/pallas_call | solution.py:396
  60.7 1.1 %copy.9 = bf16[768,1024]{1,0:T(8,128)(2,1)} copy(bf16[768,1024]{1,0:T(8,128)(2,1)S(1)} %get-tuple-element.2) | data formatting | bytes 3145728
  61.9 0.8 %copy.10 = bf16[256,1024]{1,0:T(8,128)(2,1)} copy(bf16[256,1024]{1,0:T(8,128)(2,1)S(1)} %get-tuple-element.3) | data formatting | bytes 1048576

commit v2 on v1

--- a/solution.py
+++ b/solution.py
@@ -21,18 +21,18 @@
 MESH = pl.DeviceIdType.MESH
 
 ORDER = (
-    ("C", 1, 0, 0), ("C", 3, 0, 0), ("C", 0, 1, 0), ("C", 0, 3, 0), ("I",), ("Z",), ("R",), ("W", 1, 0, 0),
+    ("C", 1, 0, 0), ("C", 3, 0, 0), ("C", 0, 1, 0), ("C", 0, 3, 0), ("I",), ("Z",), ("W", 1, 0, 0),
     ("W", 3, 0, 1), ("W", 0, 1, 0), ("W", 0, 3, 1), ("C", 2, 0, 0), ("C", 2, 0, 1), ("C", 1, 1, 0),
-    ("C", 1, 3, 0), ("C", 3, 1, 0), ("C", 3, 3, 0), ("C", 0, 2, 0), ("C", 0, 2, 1), ("T", 1, 0),
+    ("C", 1, 3, 0), ("C", 3, 1, 0), ("C", 3, 3, 0), ("C", 0, 2, 0), ("C", 0, 2, 1), ("R",), ("T", 1, 0),
     ("W", 3, 0, 0), ("W", 1, 0, 1), ("W", 0, 1, 1), ("T", 1, 1), ("W", 0, 3, 0), ("S", 1), ("W", 2, 0, 1),
     ("W", 2, 0, 0), ("T", 2, 0), ("W", 1, 1, 0), ("W", 1, 3, 0), ("W", 3, 1, 1), ("W", 3, 3, 1), ("T", 2, 1),
     ("W", 0, 2, 0), ("W", 0, 2, 1), ("S", 2), ("A", 0), ("C", 2, 1, 0), ("C", 2, 3, 0), ("C", 1, 2, 1),
     ("C", 1, 2, 0), ("C", 3, 2, 1), ("A", 2), ("C", 3, 2, 0), ("A", 4), ("T", 3, 0), ("A", 6), ("W", 3, 3, 0),
     ("A", 8), ("W", 3, 1, 0), ("A", 10), ("A", 12), ("W", 1, 3, 1), ("A", 14), ("T", 3, 1), ("W", 1, 1, 1),
     ("B", 0), ("B", 2), ("B", 4), ("S", 3), ("B", 6), ("W", 2, 3, 1), ("B", 8), ("W", 2, 1, 1), ("B", 10),
-    ("B", 12), ("T", 4, 0), ("B", 14), ("K", 3), ("W", 2, 3, 0), ("W", 2, 1, 0), ("K", -3), ("S", 4),
+    ("B", 12), ("F", 30), ("T", 4, 0), ("B", 14), ("K", 3), ("W", 2, 3, 0), ("W", 2, 1, 0), ("K", -3), ("S", 4),
     ("K", 4), ("G", 2, 1), ("W", 3, 2, 1), ("W", 1, 2, 0), ("C", 2, 2, 1), ("G", 2, 3), ("C", 2, 2, 0),
-    ("D",), ("W", 1, 2, 1), ("W", 3, 2, 0), ("G", 1, 2), ("G", 3, 2),
+    ("F", 20), ("D",), ("W", 1, 2, 1), ("W", 3, 2, 0), ("G", 1, 2), ("G", 3, 2),
 )
 
 
@@ -367,26 +367,34 @@
             d = jnp.dot(left, scaled[h], preferred_element_type=jnp.float32)
             neww[:, part] = (wbuf[p, h].astype(jnp.float32) + 0.5 * d).astype(jnp.bfloat16)
 
+    sent = []
+
+    def flush(keep):
+        for copy in list(copies.values())[len(sent):len(copies) - keep]:
+            copy.wait_send()
+            sent.append(copy)
+
     steps = {
         "W": take_w, "C": take_c, "T": take_t, "I": rest_of_own, "Z": start_z, "R": start_r,
-        "A": gather_first, "B": gather_next, "K": gather_far, "G": lambda i, j: gather(src[i, j]), "D": delta, "S": take_s,
+        "A": gather_first, "B": gather_next, "K": gather_far, "G": lambda i, j: gather(src[i, j]), "D": delta, "F": flush, "S": take_s,
     }
     for step in ORDER:
         steps[step[0]](*step[1:])
-    for s in (1, 0):
-        copies["W", 2, 2, s].wait_recv()
-
-        f = src[2, 2]
-        h = (acc[s] + jnp.dot(tbuf[f], wbuf[f, s], preferred_element_type=jnp.float32)) / math.sqrt(D)
-        keys[:, s * HALF:(s + 1) * HALF] = (jnp.maximum(h, 0.0) ** 2).astype(jnp.bfloat16)
-
-    for copy in copies.values():
-        copy.wait_send()
+    flush(12)
 
     @pl.when(p == m)
     def _():
         for copy in pieces():
             copy.wait_send()
+
+    for s in (1, 0):
+        copies["W", 2, 2, s].wait_recv()
+
+        f = src[2, 2]
+        h = (acc[s] + jnp.dot(tbuf[f], wbuf[f, s], preferred_element_type=jnp.float32)) / math.sqrt(D)
+        keys[:, s * HALF:(s + 1) * HALF] = (jnp.maximum(h, 0.0) ** 2).astype(jnp.bfloat16)
+
+    flush(0)
 
 
 def local(tokens, weight, fitness, row_factors, col_factors):

time: 62.8 us -> 62.6 us (level)
  no operation moved by 1% of the time
where the time goes in v2:
time: 62.6 us; the launch traced here: 62.5 us
  Pallas kernels  59.9 us (96%)
  local copies, waits for them, and re-layouts  1.94 us (3%)
  between operations  0.64 us (1%)
    pallas_call x1, Pallas kernels, local(): pl.pallas_call(kernel, out_shape=(pltpu.VMEM((ROWS, HID), bf), pltpu.VMEM...  59.9 us
    unnamed x2, local copies, waits for them, and re-layouts  1.94 us

profile of v2, /device:TPU:1, one launch (start us, length us, event | category | flops | bytes accessed | tf_op | source)
XLA Modules:
  0.0 62.5 jit_solution(3596923922354686611)
XLA Ops:
  0.6 59.9 %shard_map.68 = (bf16[768,1024]{1,0:T(8,128)(2,1)S(1)}, bf16[256,1024]{1,0:T(8,128)(2,1)S(1)}) custom-call(bf16[768,256]{1,0:T(8,128)(2,1)} %tok.1, bf16[256,1024]{1,0:T(8,128)(2,1)} %w.1, f32[24]{0:T(128)} %fit.1, bf16[24,4096]{1,0:T(8,128)(2,1)} %row_in.1, bf16[24,1024]{1,0:T(8,128)(2,1)} %col_in.1), custom_call_target="tpu_custom_call" | custom-call | flops 6700000256 | bytes 4000000 | tf_op jit(solution)/shard_map/pallas_call | solution.py:404
  60.6 1.1 %copy.9 = bf16[768,1024]{1,0:T(8,128)(2,1)} copy(bf16[768,1024]{1,0:T(8,128)(2,1)S(1)} %get-tuple-element.2) | data formatting | bytes 3145728
  61.7 0.8 %copy.10 = bf16[256,1024]{1,0:T(8,128)(2,1)} copy(bf16[256,1024]{1,0:T(8,128)(2,1)S(1)} %get-tuple-element.3) | data formatting | bytes 1048576
